TPU v7x, 32 devices: a whole 2x2x4 slice. The times are simulated.
32 devices in a mesh: frames: 4 (over y, core), blocks: 8 (over z, x).
Axes of the slice: x: 2, y: 2, z: 4, core: 2. Of those that a mesh axis runs over, the one named last changes fastest.
Arguments:
- traj: bfloat16 [4096, 8192], P('frames', 'blocks')
- span_offsets: int32 [4], replicated, may hold values from 0 to 256
- lag: int32 [1], replicated, may hold values from 1 to 256
- owner: int32 [36], replicated, may hold values from 0 to 7, as said below
Outputs:
- corr_inst: bfloat16 [40, 1024, 1024], P('blocks', 'frames')
- corr_lag: bfloat16 [40, 1024, 1024], P('blocks', 'frames')
Inputs may be any that keep to these rules, and one draw needn't show every extreme that they name: At most 5 pairs share one owner, and some owner has exactly 5.
All inputs are finite; a program needn't handle non-finite values.
Results may differ from a plain program's by a relative error of at most 0.0059.
Values may be sent and summed in bfloat16 or wider, within the bound.
A program may use at most 192 MiB of HBM per device.

v0:
```python
import jax
import jax.numpy as jnp
import numpy as np
from jax import lax
from jax.sharding import PartitionSpec as P

BS = 1024
SPAN = 512


eps = 1e-06


def shards(traj, span_offsets, lag, owner):
    nframes = lax.axis_size("frames")
    nblocks = lax.axis_size("blocks")
    group = lax.axis_index("frames")
    device = lax.axis_index("blocks")
    width = traj.shape[1] * nblocks
    nfeat = width // BS
    quarter = BS // nframes
    offset = jnp.sum(jnp.where(jnp.arange(nframes) == group, span_offsets, 0))
    first = lax.dynamic_slice_in_dim(traj, offset, SPAN, 0).astype(jnp.float32)
    later = lax.dynamic_slice_in_dim(traj, offset + lag[0], SPAN, 0).astype(jnp.float32)
    totals = lax.psum((jnp.sum(first, 0), jnp.sum(later, 0)), "frames")
    count = nframes * SPAN
    cent0 = (first - totals[0] / count).astype(jnp.bfloat16)
    cent1 = (later - totals[1] / count).astype(jnp.bfloat16)
    full0, full1 = (
        lax.all_gather(cent0, "blocks", axis=1, tiled=True),
        lax.all_gather(cent1, "blocks", axis=1, tiled=True),
    )
    own = lax.psum(jnp.sum(jnp.square(cent0.astype(jnp.float32)), 0), "frames")
    squares = lax.all_gather(own, "blocks", axis=0, tiled=True)
    inv = 1.0 / jnp.sqrt(squares + eps)
    rows_np, cols_np = np.triu_indices(nfeat)
    npairs = rows_np.shape[0]
    maxown = (npairs + nblocks - 1) // nblocks
    row_table = jnp.asarray(rows_np.astype(np.int32))
    col_table = jnp.asarray(cols_np.astype(np.int32))
    before = jnp.asarray(np.tril(np.ones((npairs, npairs), np.int32), -1))
    mine = owner == device
    rank = jnp.sum(before * mine.astype(jnp.int32)[None, :], 1)
    contract = (((0,), (0,)), ((), ()))

    def products(row_block, col_block):
        left0 = lax.dynamic_slice_in_dim(full0, row_block * BS, BS, 1)
        left1 = lax.dynamic_slice_in_dim(full1, row_block * BS, BS, 1)
        right0 = lax.dynamic_slice_in_dim(full0, col_block * BS, BS, 1)
        right1 = lax.dynamic_slice_in_dim(full1, col_block * BS, BS, 1)
        inst = lax.dot_general(left0, right0, contract, preferred_element_type=jnp.float32)
        lagged = lax.dot_general(left0, right1, contract, preferred_element_type=jnp.float32)
        lagged = lagged + lax.dot_general(
            left1, right0, contract, preferred_element_type=jnp.float32
        )
        return (inst, lagged)

    def nothing(row_block, col_block):
        empty = jnp.zeros((BS, BS), jnp.float32)
        return (empty, empty)

    outs_inst = []
    outs_lag = []
    indices = []
    for slot_id in range(maxown):
        selected = mine & (rank == slot_id)
        present = jnp.any(selected)
        row_block = jnp.sum(jnp.where(selected, row_table, 0))
        col_block = jnp.sum(jnp.where(selected, col_table, 0))
        indices.append((row_block, col_block, present))
    part_inst = []
    part_lag = []
    for slot_id in range(maxown):
        row_block, col_block, present = indices[slot_id]
        inst, lagged = lax.cond(present, products, nothing, row_block, col_block)
        part_inst.append(inst)
        part_lag.append(lagged)
    red_inst, red_lag = (
        lax.psum_scatter(jnp.stack(part_inst), "frames", scatter_dimension=1, tiled=True),
        lax.psum_scatter(jnp.stack(part_lag), "frames", scatter_dimension=1, tiled=True),
    )
    for slot_id in range(maxown):
        row_inv = lax.dynamic_slice_in_dim(
            inv, indices[slot_id][0] * BS + group * quarter, quarter, 0
        )
        col_inv = lax.dynamic_slice_in_dim(inv, indices[slot_id][1] * BS, BS, 0)
        normalize_inst = red_inst[slot_id] * row_inv[:, None] * col_inv[None, :]
        normalize_lagged = 0.5 * red_lag[slot_id] * row_inv[:, None] * col_inv[None, :]
        done_inst = normalize_inst.astype(jnp.bfloat16)
        done_lag = normalize_lagged.astype(jnp.bfloat16)
        outs_inst.append(done_inst)
        outs_lag.append(done_lag)
    return (jnp.stack(outs_inst), jnp.stack(outs_lag))


def solution(mesh):
    in_specs = (P("frames", "blocks"), P(), P(), P())
    out_specs = (P("blocks", "frames", None), P("blocks", "frames", None))
    return jax.shard_map(shards, mesh=mesh, in_specs=in_specs, out_specs=out_specs, check_vma=False)
```

profile of v0, /device:TPU:0, one launch (start us, length us, event | category | flops | bytes accessed | tf_op | source)
XLA Modules:
  0.0 704.1 jit_solution(5687971998011623109)
XLA Ops:
  8.0 1.3 fusion.82
  12.0 2.1 convert_reduce_fusion
  14.1 8.4 %psum.21 = f32[1024]{0:T(1024)S(1)} all-reduce(f32[1024]{0:T(1024)S(1)} %get-tuple-element.93), channel_id=1, replica_groups=mesh['frames'=4,'blocks'=8] {'frames'}, use_global_device_ids=true, to_apply=%region_5.6 | all-reduce | flops 1024 | bytes 8192 | tf_op jit(solution)/shard_map/psum | solution.py:25
  22.5 2.6 multiply_reduce_fusion
  25.1 5.8 all-reduce
  31.0 1.3 fusion.51
  37.2 0.9 select_reduce_fusion
  38.0 119.7 %all-gather.5.cloned.1.call-done = bf16[512,8192]{1,0:T(8,128)(2,1)} async-done(((bf16[512,1024]{1,0:T(8,128)(2,1)}), bf16[512,8192]{1,0:T(8,128)(2,1)}) %all-gather.5.cloned.1.call-update) | async-done | bytes 8388624 | tf_op jit(solution)/shard_map/all_gather | solution.py:31
  157.8 125.9 %all-gather.3.cloned.1.call-done = bf16[512,8192]{1,0:T(8,128)(2,1)} async-done(((bf16[512,1024]{1,0:T(8,128)(2,1)}), bf16[512,8192]{1,0:T(8,128)(2,1)}) %all-gather.3.cloned.1.call-update) | async-done | bytes 8388624 | tf_op jit(solution)/shard_map/all_gather | solution.py:30
  283.7 13.6 %conditional.5 = (f32[1,1024,1024]{2,1,0:T(8,128)}, f32[1,1024,1024]{2,1,0:T(8,128)}) conditional(s32[]{:T(128)} %convert_element_type.74, () %tuple.68, (s32[]{:T(128)}, bf16[512,8192]{1,0:T(8,128)(2,1)}, s32[]{:T(128)}, bf16[512,8192]{1,0:T(8,128)(2,1)}) %tuple.69), branch_computations={%region_9.10_spmd, %region_10.11_spmd} | conditional | flops 3222274048 | bytes 23068804 | solution.py:75
  284.9 2.8 fusion.1
  287.7 4.8 add_bitcast_fusion
  292.5 4.8 convolution_bitcast_fusion
  297.3 8.3 %constant_dynamic-update-slice_fusion.4 = (f32[5,1024,1024]{2,1,0:T(8,128)}, f32[5,1024,1024]{2,1,0:T(8,128)}) fusion(f32[1,1024,1024]{2,1,0:T(8,128)} %get-tuple-element.82, f32[1,1024,1024]{2,1,0:T(8,128)} %get-tuple-element.87), kind=kLoop, calls=%fused_computation.111 | loop fusion | bytes 16777216
  305.6 13.8 %conditional.6 = (f32[1,1024,1024]{2,1,0:T(8,128)}, f32[1,1024,1024]{2,1,0:T(8,128)}) conditional(s32[]{:T(128)} %convert_element_type.79, () %tuple.70, (s32[]{:T(128)}, bf16[512,8192]{1,0:T(8,128)(2,1)}, s32[]{:T(128)}, bf16[512,8192]{1,0:T(8,128)(2,1)}) %tuple.71), branch_computations={%region_14.15_spmd, %region_15.16_spmd} | conditional | flops 3222274048 | bytes 23068804 | solution.py:75
  306.9 2.8 fusion.11
  309.7 4.8 add_bitcast_fusion.1
  314.6 4.9 convolution_bitcast_fusion.1
  319.4 4.7 constant_dynamic-update-slice_fusion.3
  324.2 13.9 %conditional.7 = (f32[1,1024,1024]{2,1,0:T(8,128)}, f32[1,1024,1024]{2,1,0:T(8,128)}) conditional(s32[]{:T(128)} %convert_element_type.80, () %tuple.72, (s32[]{:T(128)}, bf16[512,8192]{1,0:T(8,128)(2,1)}, s32[]{:T(128)}, bf16[512,8192]{1,0:T(8,128)(2,1)}) %tuple.73), branch_computations={%region_19.20_spmd, %region_20.21_spmd} | conditional | flops 3222274048 | bytes 23068804 | solution.py:75
  325.6 2.8 fusion.21
  328.4 4.9 add_bitcast_fusion.2
  333.3 4.8 convolution_bitcast_fusion.2
  338.1 4.7 constant_dynamic-update-slice_fusion.2
  342.8 13.6 %conditional.8 = (f32[1,1024,1024]{2,1,0:T(8,128)}, f32[1,1024,1024]{2,1,0:T(8,128)}) conditional(s32[]{:T(128)} %convert_element_type.81, () %tuple.74, (s32[]{:T(128)}, bf16[512,8192]{1,0:T(8,128)(2,1)}, s32[]{:T(128)}, bf16[512,8192]{1,0:T(8,128)(2,1)}) %tuple.75), branch_computations={%region_24.25_spmd, %region_25.26_spmd} | conditional | flops 3222274048 | bytes 23068804 | solution.py:75
  344.0 2.8 fusion.31
  346.8 4.8 add_bitcast_fusion.3
  351.7 4.8 convolution_bitcast_fusion.3
  356.4 4.8 constant_dynamic-update-slice_fusion.1
  361.2 13.6 %conditional.9 = (f32[1,1024,1024]{2,1,0:T(8,128)}, f32[1,1024,1024]{2,1,0:T(8,128)}) conditional(s32[]{:T(128)} %convert_element_type.82, () %tuple.76, (s32[]{:T(128)}, bf16[512,8192]{1,0:T(8,128)(2,1)}, s32[]{:T(128)}, bf16[512,8192]{1,0:T(8,128)(2,1)}) %tuple.77), branch_computations={%region_29.30_spmd, %region_30.31_spmd} | conditional | flops 3222274048 | bytes 23068804 | solution.py:75
  362.4 2.8 fusion.41
  365.2 4.9 add_bitcast_fusion.4
  370.1 4.8 convolution_bitcast_fusion.4
  374.8 4.7 constant_dynamic-update-slice_fusion
  379.6 4.9 constant_dynamic-update-slice_fusion.8
  384.6 6.2 constant_dynamic-update-slice_fusion.7
  390.8 6.4 constant_dynamic-update-slice_fusion.6
  397.1 6.4 constant_dynamic-update-slice_fusion.5
  409.8 30.4 %all_gather.11 = f32[8192]{0:T(1024)S(1)} all-gather(f32[1024]{0:T(1024)S(1)} %get-tuple-element.115), channel_id=1, replica_groups=mesh['frames'=4,'blocks'=8] {'blocks'}, dimensions={0}, use_global_device_ids=true | all-gather | bytes 36864 | tf_op jit(solution)/shard_map/all_gather | solution.py:34
  440.3 90.6 %reduce-scatter.3.cloned.1.call-done = f32[5,256,1024]{2,1,0:T(8,128)} async-done(((f32[5,1024,1024]{2,1,0:T(8,128)}), f32[5,256,1024]{2,1,0:T(8,128)}) %reduce-scatter.3.cloned.1.call-update) | async-done | bytes 5242896 | tf_op jit(solution)/shard_map/reduce_scatter | solution.py:79
  531.0 155.8 %reduce-scatter.5.cloned.1.call-done = f32[5,256,1024]{2,1,0:T(8,128)} async-done(((f32[5,1024,1024]{2,1,0:T(8,128)}), f32[5,256,1024]{2,1,0:T(8,128)}) %reduce-scatter.5.cloned.1.call-update) | async-done | bytes 5242896 | tf_op jit(solution)/shard_map/reduce_scatter | solution.py:80
  686.8 1.9 fusion.77
  688.7 2.0 fusion.78
  690.8 1.5 fusion.79
  692.2 1.5 fusion.80
  693.7 1.5 fusion.81
  695.2 1.5 copy-done.2
  696.7 0.9 copy-done.3
  (30 shorter events, 2.0 us)
Async XLA Ops:
  7.2 23.8 %copy-start = (bf16[1024,1024]{1,0:T(8,128)(2,1)S(1)}, bf16[1024,1024]{1,0:T(8,128)(2,1)}, u32[]{:S(2)}) copy-start(bf16[1024,1024]{1,0:T(8,128)(2,1)} %param.17) | copy-start | bytes 6291460
  7.2 150.6 %all-gather.5.cloned.1.call-start = ((), (), s32[]{:S(2)}) async-start(), calls=%async_computation.3 | async-start | bytes 9437184 | tf_op jit(solution)/shard_map/all_gather | solution.py:31
  11.9 21.2 %copy-start.7 = (s32[36]{0:T(128)S(1)}, s32[36]{0:T(128)}, u32[]{:S(2)}) copy-start(s32[36]{0:T(128)} %param.20) | copy-start | bytes 436
  11.9 21.2 %copy-start.4 = (s32[36,36]{1,0:T(8,128)S(1)}, s32[36,36]{1,0:T(8,128)}, u32[]{:S(2)}) copy-start(s32[36,36]{1,0:T(8,128)} %constant.86.clone) | copy-start | bytes 15556
  11.9 25.2 %copy-start.5 = (s32[36]{0:T(128)S(1)}, s32[36]{0:T(128)}, u32[]{:S(2)}) copy-start(s32[36]{0:T(128)} %constant.84.clone) | copy-start | bytes 436
  11.9 25.2 %copy-start.6 = (s32[36]{0:T(128)S(1)}, s32[36]{0:T(128)}, u32[]{:S(2)}) copy-start(s32[36]{0:T(128)} %constant.85.clone) | copy-start | bytes 436
  32.3 251.3 %all-gather.3.cloned.1.call-start = ((), (), s32[]{:S(2)}) async-start(), calls=%async_computation.2 | async-start | bytes 9437184 | tf_op jit(solution)/shard_map/all_gather | solution.py:30
  33.1 497.9 %reduce-scatter.3.cloned.1.call-start = ((), (), s32[]{:S(2)}) async-start(), calls=%async_computation.4 | async-start | bytes 26214400 | tf_op jit(solution)/shard_map/reduce_scatter | solution.py:79
  379.6 307.2 %reduce-scatter.5.cloned.1.call-start = ((), (), s32[]{:S(2)}) async-start(), calls=%async_computation.5 | async-start | bytes 26214400 | tf_op jit(solution)/shard_map/reduce_scatter | solution.py:80
  686.8 4.0 copy-start.1
  695.2 1.5 copy-start.2
  695.2 2.3 copy-start.3
Sparse Core Ops, SparseCore 0:
  32.4 125.2 all-gather.4
  160.5 123.0 all-gather.2
  379.7 151.2 reduce-scatter.2
  533.6 153.1 reduce-scatter.4
where the time goes:
time: 705 us; the launch traced here: 704 us
  waiting for transfers between devices  493 us (70%)
  matrix products  62.3 us (9%)
  local copies, waits for them, and re-layouts  53.6 us (8%)
  blocking collectives  44.6 us (6%)
  between operations  26.7 us (4%)
  other arithmetic  17.6 us (2%)
    reduce_scatter x1, waiting for transfers between devices, shards(): lax.psum_scatter(jnp.stack(part_lag), 'frames', scatter_dimension=1, tile...  156 us
    all_gather x1, waiting for transfers between devices, shards(): lax.all_gather(cent0, 'blocks', axis=1, tiled=True)  126 us
    all_gather x1, waiting for transfers between devices, shards(): lax.all_gather(cent1, 'blocks', axis=1, tiled=True)  120 us
    reduce_scatter x1, waiting for transfers between devices, shards(): lax.psum_scatter(jnp.stack(part_inst), 'frames', scatter_dimension=1, til...  90.6 us
    unnamed x23, local copies, waits for them, and re-layouts  42.5 us
    all_gather x1, blocking collectives, shards(): squares = lax.all_gather(own, 'blocks', axis=0, tiled=True)  30.4 us
    dot_general x5, matrix products, products(): lax.dot_general(left1, right0, contract, preferred_element_type=jnp.float32)  24.2 us
    dot_general x5, matrix products, products(): lax.dot_general(left0, right0, contract, preferred_element_type=jnp.float32)  23.9 us
  transfers between devices with their start and end apart: 4, of which 4 were waited for; matrix products, arithmetic and copies ran while one was open for 4% of the time, Pallas kernels for 0%

commit v1 on v0

v1 whole, which is shorter than its diff:
```python
import functools

import jax
import jax.numpy as jnp
import numpy as np
from jax import lax
from jax.experimental import pallas as pl
from jax.experimental.pallas import tpu as pltpu
from jax.sharding import PartitionSpec as P

BS = 1024
SPAN = 512
MAXLAG = 256
WINDOW = SPAN + MAXLAG
ZX_PIECES = ((0, 320), (320, 320))
XZ_PIECE = (640, 128)
eps = 1e-06
MESH = pl.DeviceIdType.MESH


def remote(src, dst, send_sem, recv_sem, device_id):
    return pltpu.make_async_remote_copy(
        src_ref=src,
        dst_ref=dst,
        send_sem=send_sem,
        recv_sem=recv_sem,
        device_id=device_id,
        device_id_type=MESH,
    )


def gather_kernel(
    nz, lag_ref, raw_ref, gat_ref, stats_ref,
    sums, squares, send_sem, recv_sem, own_sem,
    sum_send, sum_recv, sq_send, sq_recv, st_send, st_recv,
):
    nf = lax.axis_size("frames")
    nb = 2 * nz
    group = lax.axis_index("frames")
    me = lax.axis_index("blocks")
    z, x = me // 2, me % 2
    across = z * 2 + 1 - x
    width = raw_ref.shape[1]

    barrier = pltpu.get_barrier_semaphore()
    for d in range(1, nb):
        pl.semaphore_signal(
            barrier, inc=1, device_id={"blocks": (me + d) % nb}, device_id_type=MESH
        )
    for d in range(1, nf):
        pl.semaphore_signal(
            barrier, inc=1, device_id={"frames": (group + d) % nf}, device_id_type=MESH
        )
    pl.semaphore_wait(barrier, nb + nf - 2)

    pending = []
    pieces = ZX_PIECES + (XZ_PIECE,)

    def send(cond, block, k, way, target):
        start, size = pieces[k]
        rows = pl.ds(start, size)

        def copy(src):
            return remote(
                src,
                gat_ref.at[block, rows],
                send_sem.at[way, block, k],
                recv_sem.at[block, k],
                {"blocks": target},
            )

        mine = block is me
        src = raw_ref.at[rows] if mine else gat_ref.at[block, rows]

        def go():
            copy(src).start()

        def end():
            copy(src).wait_send()

        if cond is None:
            go()
        else:
            pl.when(cond)(go)
        pending.append((cond, end))

    def arrived(block, k):
        start, size = pieces[k]
        here = gat_ref.at[block, pl.ds(start, size)]
        pltpu.make_async_copy(here, here, recv_sem.at[block, k]).wait()

    up, down = me + 2, me - 2
    send(None, me, 2, 2, across)
    for k in range(len(pieces)):
        send(z < nz - 1, me, k, 0, up)
        send(z > 0, me, k, 1, down)
        if k < 2:
            send(None, me, k, 2, across)
    own = pltpu.make_async_copy(raw_ref, gat_ref.at[me], own_sem)
    own.start()

    lag = lag_ref[0]
    chunk = 64
    zero = jnp.zeros((1, width), jnp.float32)

    def add(i, carry):
        total0, total1 = carry
        start = pl.multiple_of(i * chunk, chunk)
        values = raw_ref[pl.ds(start, chunk), :].astype(jnp.float32)
        row = start + lax.broadcasted_iota(jnp.int32, (chunk, width), 0)
        in0 = row < SPAN
        in1 = (row >= lag) & (row < lag + SPAN)
        total0 += jnp.sum(jnp.where(in0, values, 0.0), 0, keepdims=True)
        total1 += jnp.sum(jnp.where(in1, values, 0.0), 0, keepdims=True)
        return total0, total1

    total0, total1 = lax.fori_loop(0, WINDOW // chunk, add, (zero, zero))
    sums[group] = jnp.concatenate([total0, total1, jnp.zeros((6, width), jnp.float32)], 0)

    def spread(buf, ssem, rsem):
        copies = []
        for d in range(1, nf):
            other = (group + d) % nf
            copy = remote(
                buf.at[group], buf.at[group], ssem.at[d], rsem.at[d], {"frames": other}
            )
            copy.start()
            copies.append(copy)
        return copies

    sum_copies = spread(sums, sum_send, sum_recv)

    arrived(across, 2)
    send(z < nz - 1, across, 2, 0, up)
    send(z > 0, across, 2, 1, down)

    def forward(dist):
        for k in range(2):
            for side in (-1, 1):
                zb = z + side * dist
                have = (zb >= 0) if side < 0 else (zb < nz)
                block = zb * 2 + x
                on = have & ((z < nz - 1) if side < 0 else (z > 0))
                pl.when(have)(functools.partial(arrived, block, k))
                send(on, block, k, 0 if side < 0 else 1, up if side < 0 else down)
                send(have, block, k, 2, across)
        for side in (-1, 1):
            zb = z + side * dist
            have = (zb >= 0) if side < 0 else (zb < nz)
            on = have & ((z < nz - 1) if side < 0 else (z > 0))
            for block in (zb * 2 + x, zb * 2 + 1 - x):
                pl.when(have)(functools.partial(arrived, block, 2))
                send(on, block, 2, 0 if side < 0 else 1, up if side < 0 else down)

    forward(1)
    for copy in sum_copies:
        copy.wait()
    means = sums[0]
    for i in range(1, nf):
        means = means + sums[i]
    means = means / (nf * SPAN)
    mean0 = means[0:1]

    def add_squares(i, total):
        start = pl.multiple_of(i * chunk, chunk)
        values = raw_ref[pl.ds(start, chunk), :].astype(jnp.float32)
        cent = (values - mean0).astype(jnp.bfloat16).astype(jnp.float32)
        return total + jnp.sum(cent * cent, 0, keepdims=True)

    total = lax.fori_loop(0, SPAN // chunk, add_squares, zero)
    squares[group] = jnp.broadcast_to(total, (8, width))
    sq_copies = spread(squares, sq_send, sq_recv)
    forward(2)
    for copy in sq_copies:
        copy.wait()
    total = squares[0]
    for i in range(1, nf):
        total = total + squares[i]
    row = lax.broadcasted_iota(jnp.int32, (8, width), 0)
    stats_ref[me] = jnp.where(row < 2, means, total)
    st_copies = []
    for d in range(1, nb):
        copy = remote(
            stats_ref.at[me], stats_ref.at[me], st_send.at[d], st_recv.at[d],
            {"blocks": (me + d) % nb},
        )
        copy.start()
        st_copies.append(copy)
    for dist in range(3, nz):
        forward(dist)
    for k in range(2):
        arrived(across, k)
    for dist in range(1, nz):
        for side in (-1, 1):
            zb = z + side * dist
            have = (zb >= 0) if side < 0 else (zb < nz)
            for k in range(2):
                pl.when(have)(functools.partial(arrived, zb * 2 + 1 - x, k))
    for cond, end in pending:
        if cond is None:
            end()
        else:
            pl.when(cond)(end)
    for copy in st_copies:
        copy.wait()
    own.wait()


def gather_windows(raw, lag):
    nf = lax.axis_size("frames")
    nb = lax.axis_size("blocks")
    width = raw.shape[1]
    dma = pltpu.SemaphoreType.DMA
    return pl.pallas_call(
        functools.partial(gather_kernel, nb // 2),
        out_shape=(
            jax.ShapeDtypeStruct((nb, WINDOW, width), jnp.bfloat16),
            jax.ShapeDtypeStruct((nb, 8, width), jnp.float32),
        ),
        in_specs=[
            pl.BlockSpec(memory_space=pltpu.SMEM),
            pl.BlockSpec(memory_space=pltpu.VMEM),
        ],
        out_specs=(
            pl.BlockSpec(memory_space=pl.ANY),
            pl.BlockSpec(memory_space=pltpu.VMEM),
        ),
        scratch_shapes=[
            pltpu.VMEM((nf, 8, width), jnp.float32),
            pltpu.VMEM((nf, 8, width), jnp.float32),
            dma((3, nb, 3)),
            dma((nb, 3)),
            dma,
            dma((nf,)),
            dma((nf,)),
            dma((nf,)),
            dma((nf,)),
            dma((nb,)),
            dma((nb,)),
        ],
        compiler_params=pltpu.CompilerParams(
            collective_id=0, has_side_effects=True, vmem_limit_bytes=32 * 2**20
        ),
        name="gather_windows",
    )(lag, raw)


def products_kernel(
    maxown, table_ref, full0_ref, full1_ref, out_ref,
    core_send, core_recv, held, y_send, y_recv,
    cs_sem, cr_sem, ys_sem, yr_sem,
):
    group = lax.axis_index("frames")
    y, core = group // 2, group % 2
    mate = y * 2 + 1 - core
    far = (1 - y) * 2 + core
    quarter = BS // 4
    barrier = pltpu.get_barrier_semaphore()
    for other in (mate, far):
        pl.semaphore_signal(barrier, inc=1, device_id={"frames": other}, device_id_type=MESH)
    pl.semaphore_wait(barrier, 2)
    contract = (((0,), (0,)), ((), ()))

    def dot(a, b):
        return lax.dot_general(a, b, contract, preferred_element_type=jnp.float32)

    def core_copy(t, part):
        return remote(
            core_send.at[t % 4, part], core_recv.at[t, part],
            cs_sem.at[t % 4, part], cr_sem.at[t, part], {"frames": mate},
        )

    def y_copy(t):
        return remote(
            y_send.at[t % 4], y_recv.at[t], ys_sem.at[t % 4], yr_sem.at[t], {"frames": far}
        )

    def multiply(s):
        i = table_ref[0, s]
        j = table_ref[1, s]

        def part(row_quarter, store):
            cols = pl.ds(pl.multiple_of(row_quarter * quarter, quarter), quarter)
            left0 = full0_ref[i, :, cols]
            left1 = full1_ref[i, :, cols]
            store(0, dot(left0, full0_ref[j]))
            store(1, dot(left0, full1_ref[j]) + dot(left1, full0_ref[j]))

        for p, row_quarter in enumerate(((1 - y) * 2 + 1 - core, y * 2 + 1 - core)):
            def to_mate(o, value, p=p):
                t = s * 2 + o

                @pl.when(s >= 2)
                def _():
                    core_copy(t, p).wait_send()

                core_send[t % 4, p] = value.astype(jnp.bfloat16)
                core_copy(t, p).start()

            part(row_quarter, to_mate)

        def keep_far(o, value):
            held[(s % 2) * 2 + o] = value

        def keep_mine(o, value):
            out_ref[s * 2 + o] = value

        part((1 - y) * 2 + core, keep_far)
        part(y * 2 + core, keep_mine)

    def pass_on(s):
        for o in range(2):
            t = s * 2 + o
            core_copy(t, 0).wait_recv()
            core_copy(t, 1).wait_recv()

            @pl.when(s >= 2)
            def _():
                y_copy(t).wait_send()

            y_send[t % 4] = (
                held[(s % 2) * 2 + o] + core_recv[t, 0].astype(jnp.float32)
            ).astype(jnp.bfloat16)
            y_copy(t).start()
            out_ref[t] += core_recv[t, 1].astype(jnp.float32)

    def step(s, carry):
        pl.when(s < maxown)(lambda: multiply(s))
        pl.when(s >= 1)(lambda: pass_on(s - 1))
        return carry

    lax.fori_loop(0, maxown + 1, step, 0)

    def finish(t, carry):
        y_copy(t).wait_recv()
        out_ref[t] += y_recv[t].astype(jnp.float32)
        return carry

    lax.fori_loop(0, 2 * maxown, finish, 0)
    for t in range(max(0, 2 * maxown - 4), 2 * maxown):
        y_copy(t).wait_send()
        core_copy(t, 0).wait_send()
        core_copy(t, 1).wait_send()


def owned_products(table, full0, full1, maxown):
    quarter = BS // 4
    n = 2 * maxown
    dma = pltpu.SemaphoreType.DMA
    vmem = pl.BlockSpec(memory_space=pltpu.VMEM)
    return pl.pallas_call(
        functools.partial(products_kernel, maxown),
        out_shape=jax.ShapeDtypeStruct((n, quarter, BS), jnp.float32),
        in_specs=[pl.BlockSpec(memory_space=pltpu.SMEM), vmem, vmem],
        out_specs=vmem,
        scratch_shapes=[
            pltpu.VMEM((4, 2, quarter, BS), jnp.bfloat16),
            pltpu.VMEM((n, 2, quarter, BS), jnp.bfloat16),
            pltpu.VMEM((4, quarter, BS), jnp.float32),
            pltpu.VMEM((4, quarter, BS), jnp.bfloat16),
            pltpu.VMEM((n, quarter, BS), jnp.bfloat16),
            dma((4, 2)),
            dma((n, 2)),
            dma((4,)),
            dma((n,)),
        ],
        compiler_params=pltpu.CompilerParams(
            collective_id=1, has_side_effects=True, vmem_limit_bytes=60 * 2**20
        ),
        name="owned_products",
    )(table, full0, full1)


def gather_plain(raw, lag):
    nframes = lax.axis_size("frames")
    count = nframes * SPAN
    first = raw[:SPAN].astype(jnp.float32)
    later = lax.dynamic_slice_in_dim(raw, lag, SPAN, 0).astype(jnp.float32)
    means = lax.psum(jnp.stack([jnp.sum(first, 0), jnp.sum(later, 0)]), "frames") / count
    cent0 = (first - means[0]).astype(jnp.bfloat16)
    own = lax.psum(jnp.sum(jnp.square(cent0.astype(jnp.float32)), 0), "frames")
    stats = jnp.concatenate([means, own[None]], 0)
    return lax.all_gather(raw, "blocks", axis=0), lax.all_gather(stats, "blocks", axis=0)


def shards(traj, span_offsets, lag, owner):
    nframes = lax.axis_size("frames")
    nblocks = lax.axis_size("blocks")
    group = lax.axis_index("frames")
    device = lax.axis_index("blocks")
    width = traj.shape[1] * nblocks
    nfeat = width // BS
    quarter = BS // nframes
    offset = jnp.sum(jnp.where(jnp.arange(nframes) == group, span_offsets, 0))
    raw = lax.dynamic_slice_in_dim(traj, offset, WINDOW, 0)
    if nblocks == 8 and nframes == 4:
        gathered, stats = gather_windows(raw, lag)
    else:
        gathered, stats = gather_plain(raw, lag[0])
        split = (nfeat, nblocks // nfeat)
        gathered = gathered.reshape(split + gathered.shape[1:])
        gathered = jnp.swapaxes(gathered, 1, 2).reshape(nfeat, WINDOW, BS)
        stats = stats.reshape(split + stats.shape[1:])
        stats = jnp.swapaxes(stats, 1, 2).reshape(nfeat, stats.shape[2], BS)
    full0 = (gathered[:, :SPAN].astype(jnp.float32) - stats[:, 0:1]).astype(jnp.bfloat16)
    full1 = lax.dynamic_slice_in_dim(gathered, lag[0], SPAN, 1).astype(jnp.float32)
    full1 = (full1 - stats[:, 1:2]).astype(jnp.bfloat16)
    inv = 1.0 / jnp.sqrt(stats[:, 2] + eps)

    rows_np, cols_np = np.triu_indices(nfeat)
    npairs = rows_np.shape[0]
    maxown = (npairs + nblocks - 1) // nblocks
    before = jnp.asarray(np.tril(np.ones((npairs, npairs), np.int32), -1))
    mine = owner == device
    rank = jnp.sum(before * mine.astype(jnp.int32)[None, :], 1)
    selected = mine[None, :] & (rank[None, :] == jnp.arange(maxown)[:, None])
    present = jnp.any(selected, 1)
    row_block = jnp.sum(jnp.where(selected, jnp.asarray(rows_np.astype(np.int32)), 0), 1)
    col_block = jnp.sum(jnp.where(selected, jnp.asarray(cols_np.astype(np.int32)), 0), 1)
    table = jnp.stack([row_block, col_block]).astype(jnp.int32)

    total = owned_products(table, full0, full1, maxown)
    total = total.reshape(maxown, 2, quarter, BS)
    mine_inv = lax.dynamic_slice_in_dim(inv, group * quarter, quarter, 1)
    row_inv = jnp.where(present[:, None], jnp.take(mine_inv, row_block, axis=0), 0.0)
    col_inv = jnp.take(inv, col_block, axis=0)
    corr_inst = total[:, 0] * row_inv[:, :, None] * col_inv[:, None, :]
    corr_lag = 0.5 * total[:, 1] * row_inv[:, :, None] * col_inv[:, None, :]
    return (corr_inst.astype(jnp.bfloat16), corr_lag.astype(jnp.bfloat16))


def solution(mesh):
    in_specs = (P("frames", "blocks"), P(), P(), P())
    out_specs = (P("blocks", "frames", None), P("blocks", "frames", None))
    return jax.shard_map(shards, mesh=mesh, in_specs=in_specs, out_specs=out_specs, check_vma=False)
```

time: 705 us -> 302 us (0.43)
  waiting for transfers between devices: 493 us -> 0 us
  Pallas kernels: 0 us -> 267 us
  matrix products: 62.3 us -> 0 us
  local copies, waits for them, and re-layouts: 53.6 us -> 6.15 us
  blocking collectives: 44.6 us -> 0 us
  between operations: 26.7 us -> 3.5 us
    pallas_call x0 -> x2, Pallas kernels: none -> 267 us  [the longest x1 135 us: owned_products(): pl.pallas_call(functools.partial(products_kernel, maxown), out_shape=jax....]
    reduce_scatter x2 -> x0, waiting for transfers between devices: 246 us -> none  [the longest x1 156 us: shards(): lax.psum_scatter(jnp.stack(part_lag), 'frames', scatter_dimension=1, tile...]
    all_gather x2 -> x0, waiting for transfers between devices: 246 us -> none  [the longest x1 126 us: shards(): lax.all_gather(cent0, 'blocks', axis=1, tiled=True)]
    dot_general x15 -> x0, matrix products: 62.3 us -> none  [the longest x5 24.2 us: products(): lax.dot_general(left1, right0, contract, preferred_element_type=jnp.float32)]
    unnamed x23 -> x7, local copies, waits for them, and re-layouts: 42.5 us -> 4.6 us
    all_gather x1 -> x0, blocking collectives: 30.4 us -> none  [shards(): squares = lax.all_gather(own, 'blocks', axis=0, tiled=True)]
    convert_element_type x1 -> x2, other arithmetic: 1.31 us -> 19.9 us  [the longest x1 13.8 us: shards(): full1 = (full1 - stats[:, 1:2]).astype(jnp.bfloat16)]
    psum x2 -> x0, blocking collectives: 14.2 us -> none  [shards(): totals = lax.psum((jnp.sum(first, 0), jnp.sum(later, 0)), 'frames')]
  transfers between devices with their start and end apart: 4 -> 0, of which waited for: 4 -> 0; matrix products, arithmetic and copies ran while one was open for 4% -> 0% of each run, Pallas kernels for 0% -> 0%
where the time goes in v1:
time: 302 us
  Pallas kernels  267 us (88%)
  other arithmetic  24.5 us (8%)
  local copies, waits for them, and re-layouts  6.15 us (2%)
  between operations  3.5 us (1%)
    pallas_call x1, Pallas kernels, owned_products(): pl.pallas_call(functools.partial(products_kernel, maxown), out_shape=jax....  135 us
    pallas_call x1, Pallas kernels, gather_windows(): pl.pallas_call(functools.partial(gather_kernel, nb // 2), out_shape=(jax....  133 us
    convert_element_type x1, other arithmetic, shards(): full1 = (full1 - stats[:, 1:2]).astype(jnp.bfloat16)  13.8 us
    convert_element_type x1, other arithmetic, shards(): return (corr_inst.astype(jnp.bfloat16), corr_lag.astype(jnp.bfloat16))  6.1 us

profile of v1, /device:TPU:0, one launch (start us, length us, event | category | flops | bytes accessed | tf_op | source)
XLA Modules:
  0.0 301.5 jit_solution(17006638646746860731)
XLA Ops:
  0.6 0.0 copy-start
  1.5 1.3 fusion.8
  4.7 0.7 fusion.11
  5.4 0.8 multiply_reduce_fusion
  6.2 0.1 fusion.7
  6.3 0.8 select_reduce_fusion.1
  7.1 0.6 pad_add_fusion.table_ref
  7.8 0.0 copy-done
  7.8 0.4 constant_dynamic-slice_fusion.1.raw_ref
  8.2 132.9 %gather_windows.1 = (bf16[8,768,1024]{2,1,0:T(8,128)(2,1)S(1)}, f32[8,8,1024]{2,1,0:T(8,128)S(1)}) custom-call(s32[1]{0:T(128)} %copy.25.lag_ref, bf16[768,1024]{1,0:T(8,128)(2,1)S(1)} %constant_dynamic-slice_fusion.1.raw_ref), custom_call_target="tpu_custom_call" | custom-call | tf_op jit(solution)/shard_map/gather_windows/pallas_call | solution.py:214
  141.1 0.0 copy-start.1
  141.1 4.6 %copy-done.1 = bf16[8,768,1024]{2,1,0:T(8,128)(2,1)} copy-done((bf16[8,768,1024]{2,1,0:T(8,128)(2,1)}, bf16[8,768,1024]{2,1,0:T(8,128)(2,1)S(1)}, u32[]{:S(2)}) %copy-start.1) | copy-done | bytes 12582936
  145.7 0.1 add_rsqrt_fusion
  145.8 0.6 gather_fusion
  146.4 0.6 gather_fusion.1
  147.0 0.1 broadcast_select_fusion
  147.0 0.1 broadcast_multiply_fusion
  147.1 13.8 %subtract_convert_fusion = (bf16[8,512,1024]{2,1,0:T(8,128)(2,1)}, bf16[8,512,1024]{2,1,0:T(8,128)(2,1)}) fusion(f32[8,1024]{1,0:T(8,128)S(1)} %get-tuple-element.24, bf16[8,768,1024]{2,1,0:T(8,128)(2,1)} %copy-done.1, s32[]{:T(128)S(6)} %select_n.79, f32[8,1024]{1,0:T(8,128)S(1)} %bitcast.47), kind=kLoop, calls=%fused_computation.2 | loop fusion | flops 25165824 | bytes 33619972 | tf_op jit(solution)/shard_map/convert_element_type | solution.py:407
  160.9 134.5 %owned_products.1 = f32[10,256,1024]{2,1,0:T(8,128)} custom-call(s32[2,5]{1,0:T(2,128)} %pad_add_fusion.table_ref, bf16[8,512,1024]{2,1,0:T(8,128)(2,1)} %get-tuple-element.13.full0_ref, bf16[8,512,1024]{2,1,0:T(8,128)(2,1)} %get-tuple-element.12.full1_ref), custom_call_target="tpu_custom_call" | custom-call | tf_op jit(solution)/shard_map/owned_products/pallas_call | solution.py:351
  295.4 6.1 %fusion.2 = (bf16[5,256,1024]{2,1,0:T(8,128)(2,1)}, bf16[5,256,1024]{2,1,0:T(8,128)(2,1)}) fusion(f32[5,2,256,1024]{3,2,1,0:T(8,128)} %bitcast.45, f32[5,256]{1,0:T(8,128)S(1)} %get-tuple-element.8, f32[5,1024]{1,0:T(8,128)S(1)} %broadcast_select_fusion, f32[5,256]{1,0:T(8,128)S(1)} %get-tuple-element.9), kind=kLoop, calls=%fused_computation.7 | loop fusion | flops 7864320 | bytes 15759360 | tf_op jit(solution)/shard_map/convert_element_type | solution.py:429
  (8 shorter events, 0.1 us)
Async XLA Ops:
  0.6 7.1 %copy-start = (bf16[1024,1024]{1,0:T(8,128)(2,1)S(1)}, bf16[1024,1024]{1,0:T(8,128)(2,1)}, u32[]{:S(2)}) copy-start(bf16[1024,1024]{1,0:T(8,128)(2,1)} %param.7) | copy-start | bytes 6291460
  141.1 4.6 %copy-start.1 = (bf16[8,768,1024]{2,1,0:T(8,128)(2,1)}, bf16[8,768,1024]{2,1,0:T(8,128)(2,1)S(1)}, u32[]{:S(2)}) copy-start(bf16[8,768,1024]{2,1,0:T(8,128)(2,1)S(1)} %get-tuple-element.4) | copy-start | bytes 37748740

commit v2 on v1

--- a/solution.py
+++ b/solution.py
@@ -12,6 +12,7 @@
 SPAN = 512
 MAXLAG = 256
 WINDOW = SPAN + MAXLAG
+CHUNKS = 2
 ZX_PIECES = ((0, 320), (320, 320))
 XZ_PIECE = (640, 128)
 eps = 1e-06
@@ -29,18 +30,32 @@
     )
 
 
-def gather_kernel(
-    nz, lag_ref, raw_ref, gat_ref, stats_ref,
-    sums, squares, send_sem, recv_sem, own_sem,
+def shells():
+    tiles = []
+    for p in range(CHUNKS):
+        tiles += [(p, c) for c in range(p + 1)] + [(r, p) for r in range(p)]
+    return tiles
+
+
+def fused_kernel(
+    nz, maxown, lag_ref, table_ref, raw_ref, out_ref, stats_ref,
+    sums, squares, shift, left, right, prod,
+    core_send, core_recv, held, y_send, y_recv,
+    send_sem, recv_sem, own_sem,
     sum_send, sum_recv, sq_send, sq_recv, st_send, st_recv,
+    cs_sem, cr_sem, ys_sem, yr_sem, *gat,
 ):
     nf = lax.axis_size("frames")
     nb = 2 * nz
     group = lax.axis_index("frames")
     me = lax.axis_index("blocks")
     z, x = me // 2, me % 2
+    y, core = group // 2, group % 2
+    mate = y * 2 + 1 - core
+    far = (1 - y) * 2 + core
     across = z * 2 + 1 - x
-    width = raw_ref.shape[1]
+    chunk_width = raw_ref.shape[2]
+    rows = chunk_width // 4
 
     barrier = pltpu.get_barrier_semaphore()
     for d in range(1, nb):
@@ -54,29 +69,28 @@
     pl.semaphore_wait(barrier, nb + nf - 2)
 
     pending = []
+    last = len(ZX_PIECES)
     pieces = ZX_PIECES + (XZ_PIECE,)
 
-    def send(cond, block, k, way, target):
+    def send(cond, h, block, k, way, target):
         start, size = pieces[k]
-        rows = pl.ds(start, size)
-
-        def copy(src):
+        span = pl.ds(start, size)
+        src = raw_ref.at[h, span] if block is me else gat[h].at[block, span]
+
+        def copy():
             return remote(
                 src,
-                gat_ref.at[block, rows],
-                send_sem.at[way, block, k],
-                recv_sem.at[block, k],
+                gat[h].at[block, span],
+                send_sem.at[way, block, h, k],
+                recv_sem.at[block, h, k],
                 {"blocks": target},
             )
 
-        mine = block is me
-        src = raw_ref.at[rows] if mine else gat_ref.at[block, rows]
-
         def go():
-            copy(src).start()
+            copy().start()
 
         def end():
-            copy(src).wait_send()
+            copy().wait_send()
 
         if cond is None:
             go()
@@ -84,100 +98,205 @@
             pl.when(cond)(go)
         pending.append((cond, end))
 
-    def arrived(block, k):
+    def arrived(h, block, k):
         start, size = pieces[k]
-        here = gat_ref.at[block, pl.ds(start, size)]
-        pltpu.make_async_copy(here, here, recv_sem.at[block, k]).wait()
+        here = gat[h].at[block, pl.ds(start, size)]
+        pltpu.make_async_copy(here, here, recv_sem.at[block, h, k]).wait()
 
     up, down = me + 2, me - 2
-    send(None, me, 2, 2, across)
-    for k in range(len(pieces)):
-        send(z < nz - 1, me, k, 0, up)
-        send(z > 0, me, k, 1, down)
-        if k < 2:
-            send(None, me, k, 2, across)
-    own = pltpu.make_async_copy(raw_ref, gat_ref.at[me], own_sem)
-    own.start()
-
+    is_up, is_down = z < nz - 1, z > 0
+
+    def start_own(h):
+        send(None, h, me, last, 2, across)
+        for k in range(last + 1):
+            send(is_up, h, me, k, 0, up)
+            send(is_down, h, me, k, 1, down)
+            if k < last:
+                send(None, h, me, k, 2, across)
+
+    def pass_across(h):
+        arrived(h, across, last)
+        send(is_up, h, across, last, 0, up)
+        send(is_down, h, across, last, 1, down)
+
+    def forward(h, dist):
+        for k in range(last):
+            for side in (-1, 1):
+                zb = z + side * dist
+                have = (zb >= 0) if side < 0 else (zb < nz)
+                block = zb * 2 + x
+                on = have & (is_up if side < 0 else is_down)
+                pl.when(have)(functools.partial(arrived, h, block, k))
+                send(on, h, block, k, 0 if side < 0 else 1, up if side < 0 else down)
+                send(have, h, block, k, 2, across)
+        for side in (-1, 1):
+            zb = z + side * dist
+            have = (zb >= 0) if side < 0 else (zb < nz)
+            on = have & (is_up if side < 0 else is_down)
+            for block in (zb * 2 + x, zb * 2 + 1 - x):
+                pl.when(have)(functools.partial(arrived, h, block, last))
+                send(on, h, block, last, 0 if side < 0 else 1, up if side < 0 else down)
+
+    def rest(h):
+        for k in range(last):
+            arrived(h, across, k)
+        for dist in range(1, nz):
+            for side in (-1, 1):
+                zb = z + side * dist
+                have = (zb >= 0) if side < 0 else (zb < nz)
+                for k in range(last):
+                    pl.when(have)(functools.partial(arrived, h, zb * 2 + 1 - x, k))
+
+    def core_copy(p, t, part):
+        n = 2 * p + 1
+        return remote(
+            core_send.at[t % 4, part, pl.ds(0, n)],
+            core_recv.at[t, part, pl.ds(p * p, n)],
+            cs_sem.at[t % 4, part], cr_sem.at[p, t, part], {"frames": mate},
+        )
+
+    def y_copy(p, t):
+        n = 2 * p + 1
+        return remote(
+            y_send.at[t, pl.ds(0, n)], y_recv.at[t, pl.ds(p * p, n)],
+            ys_sem.at[t], yr_sem.at[p, t], {"frames": far},
+        )
+
+    tiles = shells()
+    contract = (((0,), (0,)), ((), ()))
+
+    def dot(a, b):
+        return lax.dot_general(a, b, contract, preferred_element_type=jnp.float32)
+
+    def center(block, h, target, first, second):
+        base = gat[h][block, pl.ds(0, SPAN)].astype(jnp.float32)
+        target[h, pl.ds(first, SPAN)] = (base - stats_ref[block, h, 0:1]).astype(jnp.bfloat16)
+        later = jnp.dot(shift[...], gat[h][block], preferred_element_type=jnp.float32)
+        target[h, pl.ds(second, SPAN)] = (later - stats_ref[block, h, 1:2]).astype(jnp.bfloat16)
+
+    def multiply(p, s):
+        i = table_ref[0, s]
+        j = table_ref[1, s]
+        for h in range(p + 1):
+            center(i, h, left, 0, SPAN)
+            center(j, h, right, SPAN, 0)
+
+        @pl.when(s >= 2)
+        def _():
+            for o in range(2):
+                for part in range(2):
+                    core_copy(p, s * 2 + o, part).wait_send()
+
+        for o in range(2):
+            t = s * 2 + o
+            for n in range(2 * p + 1):
+                r, c = tiles[p * p + n]
+                if o == 0:
+                    prod[...] = dot(left[r, 0:SPAN], right[c, SPAN : 2 * SPAN])
+                else:
+                    prod[...] = dot(left[r], right[c])
+
+                def quarter(q):
+                    return prod[pl.ds(pl.multiple_of(q * rows, rows), rows)]
+
+                core_send[t % 4, 0, n] = quarter((1 - y) * 2 + 1 - core).astype(jnp.bfloat16)
+                core_send[t % 4, 1, n] = quarter(y * 2 + 1 - core).astype(jnp.bfloat16)
+                held[t % 4, n] = quarter((1 - y) * 2 + core)
+                out_ref[t, p * p + n] = quarter(y * 2 + core)
+            core_copy(p, t, 0).start()
+            core_copy(p, t, 1).start()
+
+    def pass_on(p, s):
+        span = pl.ds(p * p, 2 * p + 1)
+        for o in range(2):
+            t = s * 2 + o
+            core_copy(p, t, 0).wait_recv()
+            core_copy(p, t, 1).wait_recv()
+            y_send[t, pl.ds(0, 2 * p + 1)] = (
+                held[t % 4, pl.ds(0, 2 * p + 1)] + core_recv[t, 0, span].astype(jnp.float32)
+            ).astype(jnp.bfloat16)
+            y_copy(p, t).start()
+            out_ref[t, span] += core_recv[t, 1, span].astype(jnp.float32)
+
+    def compute(p, low, high):
+        def step(s, carry):
+            pl.when(s < maxown)(lambda: multiply(p, s))
+            pl.when(s >= 1)(lambda: pass_on(p, s - 1))
+            return carry
+
+        lax.fori_loop(low, high, step, 0)
+
+    def drain(p):
+        for t in range(max(0, 2 * maxown - 4), 2 * maxown):
+            core_copy(p, t, 0).wait_send()
+            core_copy(p, t, 1).wait_send()
+        for t in range(2 * maxown):
+            y_copy(p, t).wait_send()
+
+    start_own(0)
+    own = [
+        pltpu.make_async_copy(raw_ref.at[h], gat[h].at[me], own_sem.at[h]) for h in range(CHUNKS)
+    ]
+    for copy in own:
+        copy.start()
     lag = lag_ref[0]
-    chunk = 64
-    zero = jnp.zeros((1, width), jnp.float32)
-
-    def add(i, carry):
-        total0, total1 = carry
-        start = pl.multiple_of(i * chunk, chunk)
-        values = raw_ref[pl.ds(start, chunk), :].astype(jnp.float32)
-        row = start + lax.broadcasted_iota(jnp.int32, (chunk, width), 0)
-        in0 = row < SPAN
-        in1 = (row >= lag) & (row < lag + SPAN)
-        total0 += jnp.sum(jnp.where(in0, values, 0.0), 0, keepdims=True)
-        total1 += jnp.sum(jnp.where(in1, values, 0.0), 0, keepdims=True)
-        return total0, total1
-
-    total0, total1 = lax.fori_loop(0, WINDOW // chunk, add, (zero, zero))
-    sums[group] = jnp.concatenate([total0, total1, jnp.zeros((6, width), jnp.float32)], 0)
+    step_rows = 64
+    shape = (step_rows, chunk_width)
+    zero = jnp.zeros((1, chunk_width), jnp.float32)
+    for h in range(CHUNKS):
+
+        def add(i, carry, h=h):
+            total0, total1 = carry
+            start = pl.multiple_of(i * step_rows, step_rows)
+            values = raw_ref[h, pl.ds(start, step_rows)].astype(jnp.float32)
+            row = start + lax.broadcasted_iota(jnp.int32, shape, 0)
+            in1 = (row >= lag) & (row < lag + SPAN)
+            total0 += jnp.sum(jnp.where(row < SPAN, values, 0.0), 0, keepdims=True)
+            total1 += jnp.sum(jnp.where(in1, values, 0.0), 0, keepdims=True)
+            return total0, total1
+
+        total0, total1 = lax.fori_loop(0, WINDOW // step_rows, add, (zero, zero))
+        sums[group, h] = jnp.concatenate(
+            [total0, total1, jnp.zeros((6, chunk_width), jnp.float32)], 0
+        )
 
     def spread(buf, ssem, rsem):
         copies = []
         for d in range(1, nf):
-            other = (group + d) % nf
             copy = remote(
-                buf.at[group], buf.at[group], ssem.at[d], rsem.at[d], {"frames": other}
+                buf.at[group], buf.at[group], ssem.at[d], rsem.at[d],
+                {"frames": (group + d) % nf},
             )
             copy.start()
             copies.append(copy)
         return copies
 
     sum_copies = spread(sums, sum_send, sum_recv)
-
-    arrived(across, 2)
-    send(z < nz - 1, across, 2, 0, up)
-    send(z > 0, across, 2, 1, down)
-
-    def forward(dist):
-        for k in range(2):
-            for side in (-1, 1):
-                zb = z + side * dist
-                have = (zb >= 0) if side < 0 else (zb < nz)
-                block = zb * 2 + x
-                on = have & ((z < nz - 1) if side < 0 else (z > 0))
-                pl.when(have)(functools.partial(arrived, block, k))
-                send(on, block, k, 0 if side < 0 else 1, up if side < 0 else down)
-                send(have, block, k, 2, across)
-        for side in (-1, 1):
-            zb = z + side * dist
-            have = (zb >= 0) if side < 0 else (zb < nz)
-            on = have & ((z < nz - 1) if side < 0 else (z > 0))
-            for block in (zb * 2 + x, zb * 2 + 1 - x):
-                pl.when(have)(functools.partial(arrived, block, 2))
-                send(on, block, 2, 0 if side < 0 else 1, up if side < 0 else down)
-
-    forward(1)
+    pass_across(0)
+    forward(0, 1)
     for copy in sum_copies:
         copy.wait()
-    means = sums[0]
-    for i in range(1, nf):
-        means = means + sums[i]
-    means = means / (nf * SPAN)
-    mean0 = means[0:1]
-
-    def add_squares(i, total):
-        start = pl.multiple_of(i * chunk, chunk)
-        values = raw_ref[pl.ds(start, chunk), :].astype(jnp.float32)
-        cent = (values - mean0).astype(jnp.bfloat16).astype(jnp.float32)
-        return total + jnp.sum(cent * cent, 0, keepdims=True)
-
-    total = lax.fori_loop(0, SPAN // chunk, add_squares, zero)
-    squares[group] = jnp.broadcast_to(total, (8, width))
+    means = (sums[0] + sums[1] + sums[2] + sums[3]) / (nf * SPAN)
+    for h in range(CHUNKS):
+        mean0 = means[h, 0:1]
+
+        def add_squares(i, total, h=h, mean0=mean0):
+            start = pl.multiple_of(i * step_rows, step_rows)
+            values = raw_ref[h, pl.ds(start, step_rows)].astype(jnp.float32)
+            cent = (values - mean0).astype(jnp.bfloat16).astype(jnp.float32)
+            return total + jnp.sum(cent * cent, 0, keepdims=True)
+
+        total = lax.fori_loop(0, SPAN // step_rows, add_squares, zero)
+        squares[group, h] = jnp.broadcast_to(total, (8, chunk_width))
     sq_copies = spread(squares, sq_send, sq_recv)
-    forward(2)
+    forward(0, 2)
+    if CHUNKS > 1:
+        start_own(1)
     for copy in sq_copies:
         copy.wait()
-    total = squares[0]
-    for i in range(1, nf):
-        total = total + squares[i]
-    row = lax.broadcasted_iota(jnp.int32, (8, width), 0)
-    stats_ref[me] = jnp.where(row < 2, means, total)
+    total = squares[0] + squares[1] + squares[2] + squares[3]
+    kind = lax.broadcasted_iota(jnp.int32, total.shape, 1)
+    stats_ref[me] = jnp.where(kind < 2, means, total)
     st_copies = []
     for d in range(1, nb):
         copy = remote(
@@ -186,63 +305,99 @@
         )
         copy.start()
         st_copies.append(copy)
+    source = lax.broadcasted_iota(jnp.int32, (SPAN, WINDOW), 1)
+    target = lax.broadcasted_iota(jnp.int32, (SPAN, WINDOW), 0)
+    shift[...] = jnp.where(source == target + lag, 1.0, 0.0).astype(jnp.bfloat16)
     for dist in range(3, nz):
-        forward(dist)
-    for k in range(2):
-        arrived(across, k)
-    for dist in range(1, nz):
-        for side in (-1, 1):
-            zb = z + side * dist
-            have = (zb >= 0) if side < 0 else (zb < nz)
-            for k in range(2):
-                pl.when(have)(functools.partial(arrived, zb * 2 + 1 - x, k))
+        forward(0, dist)
+    rest(0)
+    for copy in st_copies + own:
+        copy.wait()
+
+    split = maxown // 2
+    for h in range(1, CHUNKS):
+        pass_across(h)
+        forward(h, 1)
+        if h >= 2:
+            drain(h - 2)
+        compute(h - 1, 0, split)
+        forward(h, 2)
+        if h + 1 < CHUNKS:
+            start_own(h + 1)
+        compute(h - 1, split, maxown + 1)
+        for dist in range(3, nz):
+            forward(h, dist)
+        rest(h)
+    if CHUNKS > 1:
+        drain(CHUNKS - 2)
+    compute(CHUNKS - 1, 0, maxown + 1)
+
+    def finish(t, carry):
+        for p in range(CHUNKS):
+            y_copy(p, t).wait_recv()
+        out_ref[t] += y_recv[t].astype(jnp.float32)
+        return carry
+
+    lax.fori_loop(0, 2 * maxown, finish, 0)
+    drain(CHUNKS - 1)
     for cond, end in pending:
         if cond is None:
             end()
         else:
             pl.when(cond)(end)
-    for copy in st_copies:
-        copy.wait()
-    own.wait()
-
-
-def gather_windows(raw, lag):
+
+
+def fused(raw, lag, table, maxown):
     nf = lax.axis_size("frames")
     nb = lax.axis_size("blocks")
-    width = raw.shape[1]
+    width = raw.shape[2]
+    rows = width // 4
+    n, most, every = 2 * maxown, 2 * CHUNKS - 1, CHUNKS * CHUNKS
+    pieces = len(ZX_PIECES) + 1
     dma = pltpu.SemaphoreType.DMA
+    smem = pl.BlockSpec(memory_space=pltpu.SMEM)
+    vmem = pl.BlockSpec(memory_space=pltpu.VMEM)
+    bf16, f32 = jnp.bfloat16, jnp.float32
     return pl.pallas_call(
-        functools.partial(gather_kernel, nb // 2),
+        functools.partial(fused_kernel, nb // 2, maxown),
         out_shape=(
-            jax.ShapeDtypeStruct((nb, WINDOW, width), jnp.bfloat16),
-            jax.ShapeDtypeStruct((nb, 8, width), jnp.float32),
+            jax.ShapeDtypeStruct((n, every, rows, width), f32),
+            jax.ShapeDtypeStruct((nb, CHUNKS, 8, width), f32),
         ),
-        in_specs=[
-            pl.BlockSpec(memory_space=pltpu.SMEM),
-            pl.BlockSpec(memory_space=pltpu.VMEM),
-        ],
-        out_specs=(
-            pl.BlockSpec(memory_space=pl.ANY),
-            pl.BlockSpec(memory_space=pltpu.VMEM),
-        ),
+        in_specs=[smem, smem, vmem],
+        out_specs=(vmem, vmem),
         scratch_shapes=[
-            pltpu.VMEM((nf, 8, width), jnp.float32),
-            pltpu.VMEM((nf, 8, width), jnp.float32),
-            dma((3, nb, 3)),
-            dma((nb, 3)),
-            dma,
+            pltpu.VMEM((nf, CHUNKS, 8, width), f32),
+            pltpu.VMEM((nf, CHUNKS, 8, width), f32),
+            pltpu.VMEM((SPAN, WINDOW), bf16),
+            pltpu.VMEM((CHUNKS, 2 * SPAN, width), bf16),
+            pltpu.VMEM((CHUNKS, 2 * SPAN, width), bf16),
+            pltpu.VMEM((width, width), f32),
+            pltpu.VMEM((4, 2, most, rows, width), bf16),
+            pltpu.VMEM((n, 2, every, rows, width), bf16),
+            pltpu.VMEM((4, most, rows, width), f32),
+            pltpu.VMEM((n, most, rows, width), bf16),
+            pltpu.VMEM((n, every, rows, width), bf16),
+            dma((3, nb, CHUNKS, pieces)),
+            dma((nb, CHUNKS, pieces)),
+            dma((CHUNKS,)),
             dma((nf,)),
             dma((nf,)),
             dma((nf,)),
             dma((nf,)),
             dma((nb,)),
             dma((nb,)),
-        ],
+            dma((4, 2)),
+            dma((CHUNKS, n, 2)),
+            dma((n,)),
+            dma((CHUNKS, n)),
+        ]
+        + [pltpu.VMEM((nb, WINDOW, width), bf16)] * CHUNKS,
         compiler_params=pltpu.CompilerParams(
-            collective_id=0, has_side_effects=True, vmem_limit_bytes=32 * 2**20
+            collective_id=0, has_side_effects=True, vmem_limit_bytes=61 * 2**20
         ),
-        name="gather_windows",
-    )(lag, raw)
+        name="fused",
+    )(lag, table, raw)
 
 
 def products_kernel(
@@ -393,19 +548,6 @@
     quarter = BS // nframes
     offset = jnp.sum(jnp.where(jnp.arange(nframes) == group, span_offsets, 0))
     raw = lax.dynamic_slice_in_dim(traj, offset, WINDOW, 0)
-    if nblocks == 8 and nframes == 4:
-        gathered, stats = gather_windows(raw, lag)
-    else:
-        gathered, stats = gather_plain(raw, lag[0])
-        split = (nfeat, nblocks // nfeat)
-        gathered = gathered.reshape(split + gathered.shape[1:])
-        gathered = jnp.swapaxes(gathered, 1, 2).reshape(nfeat, WINDOW, BS)
-        stats = stats.reshape(split + stats.shape[1:])
-        stats = jnp.swapaxes(stats, 1, 2).reshape(nfeat, stats.shape[2], BS)
-    full0 = (gathered[:, :SPAN].astype(jnp.float32) - stats[:, 0:1]).astype(jnp.bfloat16)
-    full1 = lax.dynamic_slice_in_dim(gathered, lag[0], SPAN, 1).astype(jnp.float32)
-    full1 = (full1 - stats[:, 1:2]).astype(jnp.bfloat16)
-    inv = 1.0 / jnp.sqrt(stats[:, 2] + eps)
 
     rows_np, cols_np = np.triu_indices(nfeat)
     npairs = rows_np.shape[0]
@@ -419,7 +561,30 @@
     col_block = jnp.sum(jnp.where(selected, jnp.asarray(cols_np.astype(np.int32)), 0), 1)
     table = jnp.stack([row_block, col_block]).astype(jnp.int32)
 
-    total = owned_products(table, full0, full1, maxown)
+    if nblocks == 8 and nframes == 4:
+        lanes = quarter // CHUNKS
+        raw = raw.reshape(WINDOW, 4, CHUNKS, lanes).transpose(2, 0, 1, 3)
+        total, stats = fused(raw.reshape(CHUNKS, WINDOW, 4 * lanes), lag, table, maxown)
+        squares = stats[:, :, 2].reshape(nfeat, CHUNKS, 4, lanes)
+        squares = squares.transpose(0, 2, 1, 3).reshape(nfeat, BS)
+        order = shells()
+        order = [order.index((r, c)) for r in range(CHUNKS) for c in range(CHUNKS)]
+        total = jnp.stack([total[:, k] for k in order], 1)
+        total = total.reshape(maxown, 2, CHUNKS, CHUNKS, lanes, 4, lanes)
+        total = total.transpose(0, 1, 2, 4, 5, 3, 6)
+    else:
+        gathered, stats = gather_plain(raw, lag[0])
+        split = (nfeat, nblocks // nfeat)
+        gathered = gathered.reshape(split + gathered.shape[1:])
+        gathered = jnp.swapaxes(gathered, 1, 2).reshape(nfeat, WINDOW, BS)
+        stats = stats.reshape(split + stats.shape[1:])
+        stats = jnp.swapaxes(stats, 1, 2).reshape(nfeat, stats.shape[2], BS)
+        full0 = (gathered[:, :SPAN].astype(jnp.float32) - stats[:, 0:1]).astype(jnp.bfloat16)
+        full1 = lax.dynamic_slice_in_dim(gathered, lag[0], SPAN, 1).astype(jnp.float32)
+        full1 = (full1 - stats[:, 1:2]).astype(jnp.bfloat16)
+        squares = stats[:, 2]
+        total = owned_products(table, full0, full1, maxown)
+    inv = 1.0 / jnp.sqrt(squares + eps)
     total = total.reshape(maxown, 2, quarter, BS)
     mine_inv = lax.dynamic_slice_in_dim(inv, group * quarter, quarter, 1)
     row_inv = jnp.where(present[:, None], jnp.take(mine_inv, row_block, axis=0), 0.0)

time: 302 us -> 333 us (1.10)
  local copies, waits for them, and re-layouts: 6.15 us -> 65.7 us
  Pallas kernels: 267 us -> 241 us
    reshape x0 -> x3, local copies, waits for them, and re-layouts: none -> 30 us  [the longest x1 14.2 us: shards(): total = total.reshape(maxown, 2, quarter, BS)]
    pallas_call x2 -> x1, Pallas kernels: 267 us -> 241 us  [fused(): pl.pallas_call(functools.partial(fused_kernel, nb // 2, maxown), out_shap...]
    transpose x0 -> x2, local copies, waits for them, and re-layouts: none -> 20.8 us  [the longest x1 18.6 us: shards(): total = total.transpose(0, 1, 2, 4, 5, 3, 6)]
    convert_element_type x1 -> x0, other arithmetic: 13.8 us -> none  [shards(): full1 = (full1 - stats[:, 1:2]).astype(jnp.bfloat16)]
    another operation x0 -> x1, other arithmetic: none -> 10.2 us  [shards(): total = jnp.stack([total[:, k] for k in order], 1)]
    slice x0 -> x2, local copies, waits for them, and re-layouts: none -> 9.11 us  [shards(): total = jnp.stack([total[:, k] for k in order], 1)]
where the time goes in v2:
time: 333 us; the launch traced here: 332 us
  Pallas kernels  241 us (72%)
  local copies, waits for them, and re-layouts  65.7 us (20%)
  other arithmetic  21.8 us (7%)
  between operations  3.47 us (1%)
    pallas_call x1, Pallas kernels, fused(): pl.pallas_call(functools.partial(fused_kernel, nb // 2, maxown), out_shap...  241 us
    transpose x1, local copies, waits for them, and re-layouts, shards(): total = total.transpose(0, 1, 2, 4, 5, 3, 6)  18.6 us
    reshape x1, local copies, waits for them, and re-layouts, shards(): total = total.reshape(maxown, 2, quarter, BS)  14.2 us
    reshape x1, local copies, waits for them, and re-layouts, shards(): total = total.reshape(maxown, 2, CHUNKS, CHUNKS, lanes, 4, lanes)  12.2 us
    another operation x1, other arithmetic, shards(): total = jnp.stack([total[:, k] for k in order], 1)  10.2 us
    slice x2, local copies, waits for them, and re-layouts, shards(): total = jnp.stack([total[:, k] for k in order], 1)  9.11 us

profile of v2, /device:TPU:0, one launch (start us, length us, event | category | flops | bytes accessed | tf_op | source)
XLA Modules:
  0.0 331.6 jit_solution(7704069819224751554)
XLA Ops:
  0.6 0.0 copy-start
  1.4 1.3 fusion.8
  4.7 0.7 fusion.11
  5.3 0.8 multiply_reduce_fusion
  6.2 0.1 fusion.7
  6.3 0.8 select_reduce_fusion.1
  7.1 0.6 pad_add_fusion.table_ref
  7.8 0.0 copy-done
  7.8 1.6 constant_dynamic-slice_fusion.1
  9.4 1.7 copy.19
  11.1 2.2 copy.16
  13.3 3.6 %reshape.107.raw_ref = bf16[2,768,512]{2,1,0:T(8,128)(2,1)} reshape(bf16[2,768,4,128]{3,2,1,0:T(4,128)(2,1)} %copy.16) | data formatting | bytes 3145728 | tf_op jit(solution)/shard_map/reshape | solution.py:567
  16.9 240.7 %fused.1 = (f32[10,4,128,512]{3,2,1,0:T(8,128)}, f32[8,2,8,512]{3,2,1,0:T(8,128)}) custom-call(s32[1]{0:T(128)S(6)} %copy.20.lag_ref, s32[2,5]{1,0:T(2,128)} %pad_add_fusion.table_ref, bf16[2,768,512]{2,1,0:T(8,128)(2,1)} %reshape.107.raw_ref), custom_call_target="tpu_custom_call" | custom-call | tf_op jit(solution)/shard_map/fused/pallas_call | solution.py:361
  257.6 1.0 add_rsqrt_fusion
  258.6 0.6 gather_fusion.1
  259.2 0.6 gather_fusion
  259.8 0.1 broadcast_select_fusion
  259.8 0.1 broadcast_multiply_fusion
  259.9 0.0 copy-start.2
  259.9 6.1 %slice.22 = f32[10,2,128,512]{3,2,1,0:T(8,128)} slice(f32[10,4,128,512]{3,2,1,0:T(8,128)} %get-tuple-element.4), slice={[0:10], [1:3], [0:128], [0:512]} | slice | bytes 10485760 | tf_op jit(solution)/shard_map/slice | solution.py:572
  266.0 1.3 copy-done.2
  267.3 3.0 fusion.12
  270.3 10.2 %pad_maximum_fusion = f32[10,4,128,512]{3,2,1,0:T(8,128)} fusion(f32[10,2,128,512]{3,2,1,0:T(8,128)} %slice.22, f32[10,1,128,512]{3,2,1,0:T(8,128)} %get-tuple-element.15, f32[10,1,128,512]{3,2,1,0:T(8,128)} %get-tuple-element.14), kind=kLoop, calls=%fused_computation.2 | loop fusion | flops 5242880 | bytes 20971520 | tf_op jit(solution)/shard_map/stack | solution.py:572
  280.6 12.2 %reshape.108 = f32[5,2,2,2,128,4,128]{6,5,4,3,2,1,0:T(4,128)} reshape(f32[10,4,128,512]{3,2,1,0:T(8,128)} %pad_maximum_fusion) | data formatting | bytes 20971520 | tf_op jit(solution)/shard_map/reshape | solution.py:573
  292.8 18.6 %copy.17 = f32[5,2,2,128,4,2,128]{6,5,4,3,2,0,1:T(2,128)} copy(f32[5,2,2,128,4,2,128]{6,4,3,5,2,1,0:T(4,128)} %bitcast.38) | data formatting | bytes 20971520 | tf_op jit(solution)/shard_map/transpose | solution.py:574
  311.4 0.0 copy-start.1
  311.4 14.2 %reshape.109 = f32[5,2,256,1024]{3,2,0,1:T(8,128)} reshape(f32[5,2,2,128,4,2,128]{6,5,4,3,2,0,1:T(2,128)} %copy.17) | data formatting | bytes 20971520 | tf_op jit(solution)/shard_map/reshape | solution.py:588
  325.6 6.1 %fusion.2 = (bf16[5,256,1024]{2,1,0:T(8,128)(2,1)}, bf16[5,256,1024]{2,1,0:T(8,128)(2,1)}) fusion(f32[5,2,256,1024]{3,2,0,1:T(8,128)} %reshape.109, f32[5,256]{1,0:T(8,128)S(1)} %get-tuple-element.8, f32[5,1024]{1,0:T(8,128)S(1)} %broadcast_select_fusion, f32[5,256]{1,0:T(8,128)S(1)} %get-tuple-element.9), kind=kLoop, calls=%fused_computation.6 | loop fusion | flops 7864320 | bytes 15759360 | tf_op jit(solution)/shard_map/convert_element_type | solution.py:594
  331.6 0.0 copy-done.1
  (6 shorter events, 0.0 us)
Async XLA Ops:
  0.6 7.2 %copy-start = (bf16[1024,1024]{1,0:T(8,128)(2,1)S(1)}, bf16[1024,1024]{1,0:T(8,128)(2,1)}, u32[]{:S(2)}) copy-start(bf16[1024,1024]{1,0:T(8,128)(2,1)} %param.7) | copy-start | bytes 6291460
  259.9 7.4 %copy-start.2 = (f32[10,4,128,512]{3,2,1,0:T(8,128)S(1)}, f32[10,4,128,512]{3,2,1,0:T(8,128)}, u32[]{:S(2)}) copy-start(f32[10,4,128,512]{3,2,1,0:T(8,128)} %get-tuple-element.4) | copy-start | bytes 31457284
  311.4 20.2 %copy-start.1 = (bf16[1024,1024]{1,0:T(8,128)(2,1)S(1)}, bf16[1024,1024]{1,0:T(8,128)(2,1)}, u32[]{:S(2)}) copy-start(bf16[1024,1024]{1,0:T(8,128)(2,1)} %param.7) | copy-start | bytes 6291460

commit v3 on v2

--- a/solution.py
+++ b/solution.py
@@ -174,6 +174,13 @@
         later = jnp.dot(shift[...], gat[h][block], preferred_element_type=jnp.float32)
         target[h, pl.ds(second, SPAN)] = (later - stats_ref[block, h, 1:2]).astype(jnp.bfloat16)
 
+    def place(t, tile, value, add):
+        r, c = tiles[tile]
+        for q in range(4):
+            where = (t, pl.ds(r * rows, rows), pl.ds((q * CHUNKS + c) * rows, rows))
+            part = value[:, q * rows : (q + 1) * rows]
+            out_ref[where] = out_ref[where] + part if add else part
+
     def multiply(p, s):
         i = table_ref[0, s]
         j = table_ref[1, s]
@@ -202,7 +209,7 @@
                 core_send[t % 4, 0, n] = quarter((1 - y) * 2 + 1 - core).astype(jnp.bfloat16)
                 core_send[t % 4, 1, n] = quarter(y * 2 + 1 - core).astype(jnp.bfloat16)
                 held[t % 4, n] = quarter((1 - y) * 2 + core)
-                out_ref[t, p * p + n] = quarter(y * 2 + core)
+                place(t, p * p + n, quarter(y * 2 + core), False)
             core_copy(p, t, 0).start()
             core_copy(p, t, 1).start()
 
@@ -216,7 +223,8 @@
                 held[t % 4, pl.ds(0, 2 * p + 1)] + core_recv[t, 0, span].astype(jnp.float32)
             ).astype(jnp.bfloat16)
             y_copy(p, t).start()
-            out_ref[t, span] += core_recv[t, 1, span].astype(jnp.float32)
+            for tile in range(p * p, (p + 1) * (p + 1)):
+                place(t, tile, core_recv[t, 1, tile].astype(jnp.float32), True)
 
     def compute(p, low, high):
         def step(s, carry):
@@ -335,7 +343,8 @@
     def finish(t, carry):
         for p in range(CHUNKS):
             y_copy(p, t).wait_recv()
-        out_ref[t] += y_recv[t].astype(jnp.float32)
+        for tile in range(CHUNKS * CHUNKS):
+            place(t, tile, y_recv[t, tile].astype(jnp.float32), True)
         return carry
 
     lax.fori_loop(0, 2 * maxown, finish, 0)
@@ -361,7 +370,7 @@
     return pl.pallas_call(
         functools.partial(fused_kernel, nb // 2, maxown),
         out_shape=(
-            jax.ShapeDtypeStruct((n, every, rows, width), f32),
+            jax.ShapeDtypeStruct((n, CHUNKS * rows, CHUNKS * width), f32),
             jax.ShapeDtypeStruct((nb, CHUNKS, 8, width), f32),
         ),
         in_specs=[smem, smem, vmem],
@@ -563,15 +572,11 @@
 
     if nblocks == 8 and nframes == 4:
         lanes = quarter // CHUNKS
-        raw = raw.reshape(WINDOW, 4, CHUNKS, lanes).transpose(2, 0, 1, 3)
-        total, stats = fused(raw.reshape(CHUNKS, WINDOW, 4 * lanes), lag, table, maxown)
+        raw = [raw[:, k * lanes : (k + 1) * lanes] for k in range(4 * CHUNKS)]
+        raw = jnp.stack([jnp.concatenate(raw[h::CHUNKS], 1) for h in range(CHUNKS)])
+        total, stats = fused(raw, lag, table, maxown)
         squares = stats[:, :, 2].reshape(nfeat, CHUNKS, 4, lanes)
         squares = squares.transpose(0, 2, 1, 3).reshape(nfeat, BS)
-        order = shells()
-        order = [order.index((r, c)) for r in range(CHUNKS) for c in range(CHUNKS)]
-        total = jnp.stack([total[:, k] for k in order], 1)
-        total = total.reshape(maxown, 2, CHUNKS, CHUNKS, lanes, 4, lanes)
-        total = total.transpose(0, 1, 2, 4, 5, 3, 6)
     else:
         gathered, stats = gather_plain(raw, lag[0])
         split = (nfeat, nblocks // nfeat)

time: 333 us -> 261 us (0.78)
  local copies, waits for them, and re-layouts: 65.7 us -> 3.26 us
  other arithmetic: 21.8 us -> 13.1 us
    reshape x3 -> x0, local copies, waits for them, and re-layouts: 30 us -> none  [the longest x1 14.2 us: shards(): total = total.reshape(maxown, 2, quarter, BS)]
    transpose x2 -> x0, local copies, waits for them, and re-layouts: 20.8 us -> none  [the longest x1 18.6 us: shards(): total = total.transpose(0, 1, 2, 4, 5, 3, 6)]
    another operation x1 -> x2, other arithmetic: 10.2 us -> 1.46 us  [shards(): raw = jnp.stack([jnp.concatenate(raw[h::CHUNKS], 1) for h in range(CHUNKS)])]
    slice x2 -> x1, local copies, waits for them, and re-layouts: 9.11 us -> 2.12 us  [shards(): raw = [raw[:, k * lanes:(k + 1) * lanes] for k in range(4 * CHUNKS)]]
where the time goes in v3:
time: 261 us; the launch traced here: 260 us
  Pallas kernels  241 us (92%)
  other arithmetic  13.1 us (5%)
  between operations  3.3 us (1%)
  local copies, waits for them, and re-layouts  3.26 us (1%)
    pallas_call x1, Pallas kernels, fused(): pl.pallas_call(functools.partial(fused_kernel, nb // 2, maxown), out_shap...  241 us
    convert_element_type x1, other arithmetic, shards(): return (corr_inst.astype(jnp.bfloat16), corr_lag.astype(jnp.bfloat16))  6.17 us

profile of v3, /device:TPU:0, one launch (start us, length us, event | category | flops | bytes accessed | tf_op | source)
XLA Modules:
  0.0 260.3 jit_solution(17913878060520677514)
XLA Ops:
  1.3 1.3 fusion.8
  4.5 0.7 fusion.11
  5.2 0.8 multiply_reduce_fusion
  6.0 0.1 fusion.7
  6.1 0.8 select_reduce_fusion.1
  7.0 0.6 pad_add_fusion.table_ref
  7.6 2.1 constant_dynamic-slice_fusion
  9.7 0.2 maximum_bitcast_fusion
  9.9 1.3 pad_maximum_fusion.raw_ref
  11.2 240.6 %fused.1 = (f32[10,256,1024]{2,1,0:T(8,128)}, f32[8,2,8,512]{3,2,1,0:T(8,128)}) custom-call(s32[1]{0:T(128)S(6)} %copy.17.lag_ref, s32[2,5]{1,0:T(2,128)} %pad_add_fusion.table_ref, bf16[2,768,512]{2,1,0:T(8,128)(2,1)} %pad_maximum_fusion.raw_ref), custom_call_target="tpu_custom_call" | custom-call | tf_op jit(solution)/shard_map/fused/pallas_call | solution.py:370
  251.8 1.0 add_rsqrt_fusion
  252.9 0.6 gather_fusion.1
  253.4 0.6 gather_fusion
  254.0 0.1 broadcast_select_fusion
  254.1 0.1 broadcast_multiply_fusion
  254.1 6.2 %fusion.2 = (bf16[5,256,1024]{2,1,0:T(8,128)(2,1)}, bf16[5,256,1024]{2,1,0:T(8,128)(2,1)}) fusion(f32[5,2,256,1024]{3,2,1,0:T(8,128)} %bitcast.39, f32[5,256]{1,0:T(8,128)S(1)} %get-tuple-element.8, f32[5,1024]{1,0:T(8,128)S(1)} %broadcast_select_fusion, f32[5,256]{1,0:T(8,128)S(1)} %get-tuple-element.9), kind=kLoop, calls=%fused_computation.5 | loop fusion | flops 7864320 | bytes 15759360 | tf_op jit(solution)/shard_map/convert_element_type | solution.py:599
  (6 shorter events, 0.0 us)

commit v4 on v3

--- a/solution.py
+++ b/solution.py
@@ -282,6 +282,8 @@
     sum_copies = spread(sums, sum_send, sum_recv)
     pass_across(0)
     forward(0, 1)
+    if CHUNKS > 1:
+        start_own(1)
     for copy in sum_copies:
         copy.wait()
     means = (sums[0] + sums[1] + sums[2] + sums[3]) / (nf * SPAN)
@@ -298,8 +300,6 @@
         squares[group, h] = jnp.broadcast_to(total, (8, chunk_width))
     sq_copies = spread(squares, sq_send, sq_recv)
     forward(0, 2)
-    if CHUNKS > 1:
-        start_own(1)
     for copy in sq_copies:
         copy.wait()
     total = squares[0] + squares[1] + squares[2] + squares[3]

time: 261 us -> 261 us (level)
  no operation moved by 1% of the time
where the time goes in v4:
time: 261 us; the launch traced here: 260 us
  Pallas kernels  241 us (92%)
  other arithmetic  13.1 us (5%)
  between operations  3.3 us (1%)
  local copies, waits for them, and re-layouts  3.26 us (1%)
    pallas_call x1, Pallas kernels, fused(): pl.pallas_call(functools.partial(fused_kernel, nb // 2, maxown), out_shap...  241 us
    convert_element_type x1, other arithmetic, shards(): return (corr_inst.astype(jnp.bfloat16), corr_lag.astype(jnp.bfloat16))  6.17 us

profile of v4, /device:TPU:0, one launch (start us, length us, event | category | flops | bytes accessed | tf_op | source)
XLA Modules:
  0.0 260.3 jit_solution(12878437837024301963)
XLA Ops:
  1.3 1.3 fusion.8
  4.5 0.7 fusion.11
  5.2 0.8 multiply_reduce_fusion
  6.0 0.1 fusion.7
  6.1 0.8 select_reduce_fusion.1
  7.0 0.6 pad_add_fusion.table_ref
  7.6 2.1 constant_dynamic-slice_fusion
  9.7 0.2 maximum_bitcast_fusion
  9.9 1.3 pad_maximum_fusion.raw_ref
  11.2 240.6 %fused.1 = (f32[10,256,1024]{2,1,0:T(8,128)}, f32[8,2,8,512]{3,2,1,0:T(8,128)}) custom-call(s32[1]{0:T(128)S(6)} %copy.17.lag_ref, s32[2,5]{1,0:T(2,128)} %pad_add_fusion.table_ref, bf16[2,768,512]{2,1,0:T(8,128)(2,1)} %pad_maximum_fusion.raw_ref), custom_call_target="tpu_custom_call" | custom-call | tf_op jit(solution)/shard_map/fused/pallas_call | solution.py:370
  251.8 1.0 add_rsqrt_fusion
  252.9 0.6 gather_fusion.1
  253.4 0.6 gather_fusion
  254.0 0.1 broadcast_select_fusion
  254.1 0.1 broadcast_multiply_fusion
  254.1 6.2 %fusion.2 = (bf16[5,256,1024]{2,1,0:T(8,128)(2,1)}, bf16[5,256,1024]{2,1,0:T(8,128)(2,1)}) fusion(f32[5,2,256,1024]{3,2,1,0:T(8,128)} %bitcast.39, f32[5,256]{1,0:T(8,128)S(1)} %get-tuple-element.8, f32[5,1024]{1,0:T(8,128)S(1)} %broadcast_select_fusion, f32[5,256]{1,0:T(8,128)S(1)} %get-tuple-element.9), kind=kLoop, calls=%fused_computation.5 | loop fusion | flops 7864320 | bytes 15759360 | tf_op jit(solution)/shard_map/convert_element_type | solution.py:599
  (6 shorter events, 0.0 us)
